TPU v7x, 512 devices: a whole 4x8x8 slice. The times are simulated.
512 devices in a mesh: slab: 64 (over z, y), plane: 8 (over x, core).
Axes of the slice: x: 4, y: 8, z: 8, core: 2. Of those that a mesh axis runs over, the one named last changes fastest.
Arguments:
- density: float32 [2, 16, 512, 8192], P(None, 'plane', None, 'slab'), may hold values from -14 to 14
- green: float32 [16, 512, 8192], P('plane', 'slab'), may hold values from -2.5 to -0.15
Outputs:
- potential: float32 [2, 16, 512, 8192], P(None, 'plane', None, 'slab')
- energy: float32 [512], P('slab')
All inputs are finite; a program needn't handle non-finite values.
Results may differ from a plain program's by a relative error of at most 0.00013.
Values sent between devices are 32-bit elements; how exact they have to be, the bound alone decides.
No kernel may reach another device: no remote copies, remote signals or barrier semaphores. Data moves between devices by JAX's collectives and lax.ppermute only.
A program may use at most 64 MiB of HBM per device.

v0:
```python
from functools import partial
import math

import jax
import jax.numpy as jnp
from jax import lax
from jax.sharding import PartitionSpec as P


def wave_table(rows, cols, size, sign):
    product = (
        jnp.arange(rows, dtype=jnp.int32)[:, None]
        * jnp.arange(cols, dtype=jnp.int32)[None, :]
        % size
    )
    angle = sign * 2.0 * math.pi / size * product.astype(jnp.float32)
    return (jnp.cos(angle), jnp.sin(angle))


def complex_product(form, left_real, left_imag, right_real, right_imag):
    multiply = partial(jnp.einsum, form, precision=lax.Precision.HIGHEST)
    out_real = multiply(left_real, right_real) - multiply(left_imag, right_imag)
    out_imag = multiply(left_real, right_imag) + multiply(left_imag, right_real)
    return (out_real, out_imag)


def block_matrix(cos_part, sin_part, sign):
    upper = jnp.concatenate([cos_part, -sign * sin_part], axis=1)
    lower = jnp.concatenate([sign * sin_part, cos_part], axis=1)
    return jnp.concatenate([upper, lower], axis=0)


def shards(density, green):
    slab_count = lax.axis_size("slab")
    local_x = density.shape[3]
    length = local_x * slab_count
    plane_local = density.shape[1]
    planes_all = plane_local * lax.axis_size("plane")
    inner_real, inner_imag = wave_table(local_x, local_x, local_x, -1.0)
    lines_all = density.shape[2]
    reordered = jnp.transpose(density, (1, 2, 0, 3)).reshape(plane_local, lines_all, 2, 1, local_x)
    moved = lax.all_to_all(reordered, "slab", split_axis=1, concat_axis=3, tiled=True)
    line_local = moved.shape[1]
    stacked = moved.reshape(plane_local, line_local, 2 * slab_count, local_x)
    outer_real, outer_imag = wave_table(slab_count, slab_count, slab_count, -1.0)
    forward_matrix = block_matrix(outer_real, outer_imag, 1.0)
    inverse_matrix = block_matrix(outer_real, outer_imag, -1.0)
    twist_real, twist_imag = wave_table(slab_count, local_x, length, -1.0)
    mixed = jnp.matmul(forward_matrix, stacked, precision=lax.Precision.HIGHEST)
    mixed = mixed.reshape(plane_local, line_local, 2, slab_count, local_x)
    real_part = mixed[:, :, 0] * twist_real - mixed[:, :, 1] * twist_imag
    imag_part = mixed[:, :, 0] * twist_imag + mixed[:, :, 1] * twist_real
    spec_real, spec_imag = complex_product(
        "bycj,ja->byca", real_part, imag_part, inner_real, inner_imag
    )
    kernel = jnp.swapaxes(green.reshape(plane_local, line_local, local_x, slab_count), 2, 3)
    energy_part = jnp.sum(kernel * (spec_real * spec_real + spec_imag * spec_imag), axis=(0, 2, 3))
    real_part, imag_part = complex_product(
        "byca,aj->bycj", kernel * spec_real, kernel * spec_imag, inner_real, -inner_imag
    )
    back = jnp.stack(
        [
            real_part * twist_real + imag_part * twist_imag,
            imag_part * twist_real - real_part * twist_imag,
        ],
        axis=2,
    )
    back = back.reshape(plane_local, line_local, 2 * slab_count, local_x)
    result = jnp.matmul(inverse_matrix, back, precision=lax.Precision.HIGHEST) * (1.0 / length)
    result = result.reshape(plane_local, line_local, 2, slab_count, local_x)
    returned = lax.all_to_all(result, "slab", split_axis=3, concat_axis=1, tiled=True)
    potential = jnp.transpose(returned.reshape(plane_local, lines_all, 2, local_x), (2, 0, 1, 3))
    energy = lax.psum(energy_part, "plane") / (length * length * planes_all)
    return (potential, energy)


def solution(mesh):
    placed = (P(None, "plane", None, "slab"), P("plane", "slab", None))
    return jax.shard_map(
        shards,
        mesh=mesh,
        in_specs=placed,
        out_specs=(P(None, "plane", None, "slab"), P("slab")),
        check_vma=False,
    )
```

profile of v0, /device:TPU:6, one launch (start us, length us, event | category | flops | bytes accessed | tf_op | source)
XLA Modules:
  0.0 97.9 jit_solution(2350084865013540904)
XLA Ops:
  0.6 3.0 %copy.41 = f32[2,2,512,128]{3,1,0,2:T(2,128)} copy(f32[2,2,512,128]{3,2,1,0:T(8,128)} %param.2) | data formatting | bytes 2097152 | tf_op args[0]
  3.6 0.0 copy-start
  3.6 16.7 %all-to-all-start = ((f32[2,512,2,1,128]{4,0,2,3,1:T(2,128)}), f32[2,512,2,1,128]{4,0,2,3,1:T(2,128)S(1)}, u32[]{:S(2)}, u32[]{:S(2)}) async-start(f32[2,512,2,1,128]{4,0,2,3,1:T(2,128)} %bitcast.107), calls=%async_computation | async-start | bytes 2097152 | tf_op jit(solution)/shard_map/all_to_all | solution.py:42
  20.4 0.0 copy-done
  20.4 0.4 reshape.63
  20.8 0.3 copy.21
  21.1 0.1 fusion.57
  21.3 0.1 broadcast_multiply_fusion
  21.4 0.1 fusion.54
  21.6 28.6 %all-to-all-done = f32[2,512,2,1,128]{4,0,2,3,1:T(2,128)S(1)} async-done(((f32[2,512,2,1,128]{4,0,2,3,1:T(2,128)}), f32[2,512,2,1,128]{4,0,2,3,1:T(2,128)S(1)}, u32[]{:S(2)}, u32[]{:S(2)}) %all-to-all-start) | async-done | bytes 1048608 | tf_op jit(solution)/shard_map/all_to_all | solution.py:42
  50.1 0.6 copy.23
  50.8 1.0 %fusion.10 = f32[128,2,8,128]{3,0,2,1:T(8,128)S(1)} fusion(f32[2,8,128,128]{3,2,1,0:T(8,128)S(1)} %bitcast.115, f32[64,64]{1,0:T(8,128)S(1)} %fusion.57, f32[64,64]{1,0:T(8,128)S(1)} %get-tuple-element.9, f32[64,64]{1,0:T(8,128)S(1)} %get-tuple-element.8), kind=kOutput, calls=%fused_computation.33 | convolution fusion | flops 402702336 | bytes 2146304 | tf_op jit(solution)/shard_map/dot_general | solution.py:49
  51.8 0.8 fusion.4
  52.6 0.8 fusion.3
  53.5 0.8 convolution_subtract_fusion.1
  54.3 0.8 fusion.1
  55.1 0.8 fusion.2
  55.9 1.0 fusion
  56.9 0.8 convolution_add_fusion
  57.7 0.9 add_bitcast_fusion
  58.6 0.1 pad_maximum_fusion
  58.7 0.1 copy.26
  58.8 1.1 %convolution_multiply_fusion = f32[128,2,8,128]{3,0,2,1:T(8,128)S(1)} fusion(f32[2,8,128,128]{3,2,1,0:T(8,128)S(1)} %bitcast.113, f32[64,64]{1,0:T(8,128)S(1)} %fusion.57, f32[64,64]{1,0:T(8,128)S(1)} %get-tuple-element.8, f32[64,64]{1,0:T(8,128)S(1)} %get-tuple-element.9), kind=kOutput, calls=%fused_computation | convolution fusion | flops 402964480 | bytes 2146304 | tf_op jit(solution)/shard_map/dot_general | solution.py:69
  59.9 1.8 %copy.27 = f32[2,8,2,64,128]{4,2,1,0,3:T(2,128)} copy(f32[2,8,2,64,128]{4,3,2,1,0:T(8,128)S(1)} %bitcast.114) | data formatting | bytes 2097152 | tf_op jit(solution)/shard_map/reshape | solution.py:70
  61.7 6.4 %all-to-all-start.1 = ((f32[2,8,2,64,128]{4,2,1,0,3:T(2,128)}), f32[2,8,2,64,128]{4,2,1,0,3:T(2,128)S(1)}, u32[]{:S(2)}, u32[]{:S(2)}) async-start(f32[2,8,2,64,128]{4,2,1,0,3:T(2,128)} %copy.27), calls=%async_computation.1 | async-start | bytes 2097152 | tf_op jit(solution)/shard_map/all_to_all | solution.py:71
  68.1 10.6 %psum.7 = f32[8]{0:T(128)S(1)} all-reduce(f32[8]{0:T(128)S(1)} %get-tuple-element.6), channel_id=1, replica_groups=mesh['slab'=64,'plane'=8] {'plane'}, use_global_device_ids=true, to_apply=%region_1.2 | all-reduce | flops 8 | bytes 64 | tf_op jit(solution)/shard_map/psum | solution.py:73
  78.7 0.5 broadcast_multiply_fusion.1
  79.2 17.6 %all-to-all-done.1 = f32[2,8,2,64,128]{4,2,1,0,3:T(2,128)S(1)} async-done(((f32[2,8,2,64,128]{4,2,1,0,3:T(2,128)}), f32[2,8,2,64,128]{4,2,1,0,3:T(2,128)S(1)}, u32[]{:S(2)}, u32[]{:S(2)}) %all-to-all-start.1) | async-done | bytes 1048608 | tf_op jit(solution)/shard_map/all_to_all | solution.py:71
  96.8 1.0 %copy.40 = f32[2,8,2,64,128]{4,1,3,0,2:T(8,128)} copy(f32[2,8,2,64,128]{4,2,1,0,3:T(2,128)S(1)} %all-to-all-done.1) | data formatting | bytes 2097152 | tf_op jit(solution)/shard_map/transpose | solution.py:72
Async XLA Ops:
  3.6 16.7 %copy-start = (f32[2,8,8192]{2,1,0:T(8,128)S(1)}, f32[2,8,8192]{2,1,0:T(8,128)}, u32[]{:S(2)}) copy-start(f32[2,8,8192]{2,1,0:T(8,128)} %param.3) | copy-start | bytes 1572868
  3.6 46.5 %all-to-all-start = ((f32[2,512,2,1,128]{4,0,2,3,1:T(2,128)}), f32[2,512,2,1,128]{4,0,2,3,1:T(2,128)S(1)}, u32[]{:S(2)}, u32[]{:S(2)}) async-start(f32[2,512,2,1,128]{4,0,2,3,1:T(2,128)} %bitcast.107), calls=%async_computation | async-start | bytes 2097152 | tf_op jit(solution)/shard_map/all_to_all | solution.py:42
  61.7 35.2 %all-to-all-start.1 = ((f32[2,8,2,64,128]{4,2,1,0,3:T(2,128)}), f32[2,8,2,64,128]{4,2,1,0,3:T(2,128)S(1)}, u32[]{:S(2)}, u32[]{:S(2)}) async-start(f32[2,8,2,64,128]{4,2,1,0,3:T(2,128)} %copy.27), calls=%async_computation.1 | async-start | bytes 2097152 | tf_op jit(solution)/shard_map/all_to_all | solution.py:71
where the time goes:
time: 98.2 us; the launch traced here: 97.9 us
  waiting for transfers between devices  46.2 us (47%)
  starting transfers between devices  23.1 us (24%)
  blocking collectives  10.6 us (11%)
  matrix products  8.83 us (9%)
  local copies, waits for them, and re-layouts  7.27 us (7%)
  other arithmetic  1.05 us (1%)
    all_to_all x1, waiting for transfers between devices, shards(): lax.all_to_all(reordered, 'slab', split_axis=1, concat_axis=3, tiled=True)  28.6 us
    all_to_all x1, waiting for transfers between devices, shards(): lax.all_to_all(result, 'slab', split_axis=3, concat_axis=1, tiled=True)  17.6 us
    all_to_all x1, starting transfers between devices, shards(): lax.all_to_all(reordered, 'slab', split_axis=1, concat_axis=3, tiled=True)  16.7 us
    psum x1, blocking collectives, shards(): energy = lax.psum(energy_part, 'plane') / (length * length * planes_all)  10.6 us
    all_to_all x1, starting transfers between devices, shards(): lax.all_to_all(result, 'slab', split_axis=3, concat_axis=1, tiled=True)  6.4 us
    dot_general x4, matrix products, complex_product(): out_imag = multiply(left_real, right_imag) + multiply(left_imag, right_real)  3.41 us
    dot_general x4, matrix products, complex_product(): out_real = multiply(left_real, right_real) - multiply(left_imag, right_imag)  3.32 us
    unnamed x3, local copies, waits for them, and re-layouts  3.01 us
  transfers between devices with their start and end apart: 2, of which 2 were waited for; matrix products, arithmetic and copies ran while one was open for 2% of the time, Pallas kernels for 0%

commit v1 on v0

v1 whole, which is shorter than its diff:
```python
import math

import numpy as np
import ml_dtypes

import jax
import jax.numpy as jnp
from jax import lax
from jax.experimental import pallas as pl
from jax.experimental.pallas import tpu as pltpu
from jax.sharding import PartitionSpec as P


def split_constant(table):
    high = table.astype(np.float32).astype(ml_dtypes.bfloat16)
    low = (table - high.astype(np.float64)).astype(np.float32).astype(ml_dtypes.bfloat16)
    return high, low


def waves(rows, cols, size):
    product = np.outer(np.arange(rows), np.arange(cols)) % size
    angle = 2.0 * math.pi / size * product
    return np.cos(angle), np.sin(angle)


def constant_tables(outer, inner):
    length = outer * inner
    cos_o, sin_o = waves(outer, outer, outer)
    mix = np.zeros((2, outer, outer, 2))
    mix[0, :, :, 0] = cos_o
    mix[0, :, :, 1] = sin_o
    mix[1, :, :, 0] = -sin_o
    mix[1, :, :, 1] = cos_o
    forward = mix.reshape(2 * outer, 2 * outer)
    unmix = np.zeros((outer, 2, 2, outer))
    unmix[:, 0, 0, :] = cos_o
    unmix[:, 0, 1, :] = -sin_o
    unmix[:, 1, 0, :] = sin_o
    unmix[:, 1, 1, :] = cos_o
    inverse = unmix.reshape(2 * outer, 2 * outer) / length
    cos_i, sin_i = waves(inner, inner, inner)
    spread = np.block([[cos_i, -sin_i], [sin_i, cos_i]])
    gather = np.block([[cos_i, sin_i], [-sin_i, cos_i]])
    tables = []
    for matrix in (forward, inverse):
        high, low = split_constant(matrix)
        tables.append(np.block([[high, high], [low, low]]))
    for matrix in (spread, gather):
        tables.extend(split_constant(matrix))
    cos_t, sin_t = waves(outer, inner, length)
    tables.append(cos_t.astype(np.float32))
    tables.append(sin_t.astype(np.float32))
    return tables


def halves(value):
    high = value.astype(jnp.bfloat16)
    low = (value - high.astype(jnp.float32)).astype(jnp.bfloat16)
    return high, low


def matmul(left, right):
    return jnp.dot(left, right, preferred_element_type=jnp.float32)


def line_kernel(
    lines_ref, green_ref, fwd_ref, inv_ref, sp_hi, sp_lo, ga_hi, ga_lo, cos_ref, sin_ref,
    out_ref, energy_ref,
):
    outer, inner = cos_ref.shape
    count = green_ref.shape[0] // outer
    rows = 2 * outer
    cos_t, sin_t = cos_ref[...], sin_ref[...]
    pair_count = 2
    for first in range(0, count, pair_count):
        group = range(first, first + pair_count)
        block = jnp.concatenate(
            [lines_ref[pl.ds(line, rows, stride=count), :] for line in group], axis=1
        )
        mixed = matmul(fwd_ref[...], jnp.concatenate(halves(block), axis=0))
        mixed = mixed[:rows] + mixed[rows:]
        turned = []
        for n in range(pair_count):
            real = mixed[:outer, n * inner:(n + 1) * inner]
            imag = mixed[outer:, n * inner:(n + 1) * inner]
            turned.append(
                jnp.concatenate(
                    [real * cos_t + imag * sin_t, imag * cos_t - real * sin_t], axis=1
                )
            )
        high, low = halves(jnp.concatenate(turned, axis=0))
        spectrum = matmul(high, sp_hi[...]) + matmul(low, sp_hi[...]) + matmul(high, sp_lo[...])
        real, imag = spectrum[:, :inner], spectrum[:, inner:]
        green = green_ref[first * outer:(first + pair_count) * outer, :]
        weighted_real, weighted_imag = green * real, green * imag
        power = weighted_real * real + weighted_imag * imag
        for n, line in enumerate(group):
            energy_ref[line:line + 1, :] = jnp.sum(
                power[n * outer:(n + 1) * outer], axis=0, keepdims=True
            )
        high, low = halves(jnp.concatenate([weighted_real, weighted_imag], axis=1))
        back = matmul(high, ga_hi[...]) + matmul(low, ga_hi[...]) + matmul(high, ga_lo[...])
        stacked = []
        for n in range(pair_count):
            real = back[n * outer:(n + 1) * outer, :inner]
            imag = back[n * outer:(n + 1) * outer, inner:]
            stacked.append(
                jnp.concatenate(
                    [real * cos_t - imag * sin_t, imag * cos_t + real * sin_t], axis=0
                )
            )
        block = jnp.concatenate(stacked, axis=1)
        result = matmul(inv_ref[...], jnp.concatenate(halves(block), axis=0))
        result = result[:rows] + result[rows:]
        for n, line in enumerate(group):
            out_ref[pl.ds(line, rows, stride=count), :] = result[:, n * inner:(n + 1) * inner]


def convolve_lines(lines, green, tables):
    vmem = pl.BlockSpec(memory_space=pltpu.VMEM)
    count = green.shape[0] // tables[-1].shape[0]
    return pl.pallas_call(
        line_kernel,
        out_shape=(
            jax.ShapeDtypeStruct(lines.shape, jnp.float32),
            jax.ShapeDtypeStruct((count, lines.shape[1]), jnp.float32),
        ),
        in_specs=[vmem] * (2 + len(tables)),
        out_specs=(vmem, vmem),
        compiler_params=pltpu.CompilerParams(vmem_limit_bytes=24 * 1024 * 1024),
        cost_estimate=pl.CostEstimate(
            flops=16 * 10 * 256**3 * 2, bytes_accessed=4 * 1024 * 1024, transcendentals=0
        ),
    )(lines, green, *tables)


def shards(density, green):
    slab_count = lax.axis_size("slab")
    parts, plane_local, lines_all, local_x = density.shape
    length = local_x * slab_count
    planes_all = plane_local * lax.axis_size("plane")
    line_local = lines_all // slab_count
    tables = [jnp.asarray(t) for t in constant_tables(slab_count, local_x)]
    tiles = density.reshape(parts, plane_local, slab_count, line_local, local_x)
    sent = jnp.transpose(tiles, (2, 0, 1, 3, 4))
    moved = lax.all_to_all(sent, "slab", split_axis=0, concat_axis=0, tiled=True)
    kernels = jnp.swapaxes(green.reshape(plane_local, line_local, local_x, slab_count), 2, 3)
    result, energy = convolve_lines(
        moved.reshape(slab_count * parts * plane_local * line_local, local_x),
        kernels.reshape(plane_local * line_local * slab_count, local_x),
        tables,
    )
    result = result.reshape(slab_count, parts, plane_local, line_local, local_x)
    returned = lax.all_to_all(result, "slab", split_axis=0, concat_axis=0, tiled=True)
    potential = jnp.transpose(returned, (1, 2, 0, 3, 4)).reshape(density.shape)
    energy = jnp.sum(energy.reshape(plane_local, line_local, local_x), axis=(0, 2))
    energy = lax.psum(energy, "plane") / (length * length * planes_all)
    return (potential, energy)


def solution(mesh):
    placed = (P(None, "plane", None, "slab"), P("plane", "slab", None))
    return jax.shard_map(
        shards,
        mesh=mesh,
        in_specs=placed,
        out_specs=(P(None, "plane", None, "slab"), P("slab")),
        check_vma=False,
    )
```

time: 98.2 us -> 91.5 us (0.932)
  matrix products: 8.83 us -> 0 us
  Pallas kernels: 0 us -> 5.4 us
  waiting for transfers between devices: 46.2 us -> 44.1 us
    dot_general x10 -> x0, matrix products: 8.83 us -> none  [the longest x4 3.41 us: complex_product(): out_imag = multiply(left_real, right_imag) + multiply(left_imag, right_real)]
    pallas_call x0 -> x1, Pallas kernels: none -> 5.4 us  [convolve_lines(): pl.pallas_call(line_kernel, out_shape=(jax.ShapeDtypeStruct(lines.shape,...]
    all_to_all x2, waiting for transfers between devices: 46.2 us -> 44.1 us  [the longest x1 26.7 us: shards(): lax.all_to_all(sent, 'slab', split_axis=0, concat_axis=0, tiled=True)]
    unnamed x3 -> x20, local copies, waits for them, and re-layouts: 3.01 us -> 1.27 us
    transpose x1 -> x2, local copies, waits for them, and re-layouts: 1.04 us -> 2.74 us  [the longest x1 1.62 us: shards(): jnp.swapaxes(green.reshape(plane_local, line_local, local_x, slab_count),...]
  transfers between devices with their start and end apart: 2 -> 2, of which waited for: 2 -> 2; matrix products, arithmetic and copies ran while one was open for 2% -> 4% of each run, Pallas kernels for 0% -> 0%
where the time goes in v1:
time: 91.5 us; the launch traced here: 91.1 us
  waiting for transfers between devices  44.1 us (48%)
  starting transfers between devices  23.1 us (25%)
  blocking collectives  10.6 us (12%)
  local copies, waits for them, and re-layouts  6.52 us (7%)
  Pallas kernels  5.4 us (6%)
    all_to_all x1, waiting for transfers between devices, shards(): lax.all_to_all(sent, 'slab', split_axis=0, concat_axis=0, tiled=True)  26.7 us
    all_to_all x1, waiting for transfers between devices, shards(): lax.all_to_all(result, 'slab', split_axis=0, concat_axis=0, tiled=True)  17.4 us
    all_to_all x1, starting transfers between devices, shards(): lax.all_to_all(sent, 'slab', split_axis=0, concat_axis=0, tiled=True)  16.7 us
    psum x1, blocking collectives, shards(): energy = lax.psum(energy, 'plane') / (length * length * planes_all)  10.6 us
    all_to_all x1, starting transfers between devices, shards(): lax.all_to_all(result, 'slab', split_axis=0, concat_axis=0, tiled=True)  6.41 us
    pallas_call x1, Pallas kernels, convolve_lines(): pl.pallas_call(line_kernel, out_shape=(jax.ShapeDtypeStruct(lines.shape,...  5.4 us
  transfers between devices with their start and end apart: 2, of which 2 were waited for; matrix products, arithmetic and copies ran while one was open for 4% of the time, Pallas kernels for 0%

profile of v1, /device:TPU:6, one launch (start us, length us, event | category | flops | bytes accessed | tf_op | source)
XLA Modules:
  0.0 91.1 jit_solution(12224714754388158282)
XLA Ops:
  0.6 0.0 copy-start
  0.6 1.2 %copy-done = f32[2,2,512,128]{3,2,1,0:T(8,128)S(1)} copy-done((f32[2,2,512,128]{3,2,1,0:T(8,128)S(1)}, f32[2,2,512,128]{3,2,1,0:T(8,128)}, u32[]{:S(2)}) %copy-start) | copy-done | bytes 1048600
  1.9 1.1 %copy_bitcast_fusion.1 = f32[64,2,2,8,128]{4,3,2,1,0:T(8,128)} fusion(f32[2,2,512,128]{3,2,1,0:T(8,128)S(1)} %copy-done), kind=kLoop, calls=%fused_computation.1 | loop fusion | bytes 2097152 | tf_op jit(solution)/shard_map/transpose | solution.py:145
  3.0 0.0 copy-start.9
  3.0 16.7 %all-to-all-start = ((f32[64,2,2,8,128]{4,3,2,1,0:T(8,128)}), f32[64,2,2,8,128]{4,3,2,1,0:T(8,128)S(1)}, u32[]{:S(2)}, u32[]{:S(2)}) async-start(f32[64,2,2,8,128]{4,3,2,1,0:T(8,128)} %copy_bitcast_fusion.1), calls=%async_computation | async-start | bytes 2097152 | tf_op jit(solution)/shard_map/all_to_all | solution.py:146
  19.7 0.0 copy-done.9
  19.7 1.4 %reshape.26 = f32[2,8,128,64]{3,2,1,0:T(8,128)} reshape(f32[2,8,8192]{2,1,0:T(8,128)S(1)} %copy-done.9) | data formatting | bytes 1048576 | tf_op jit(solution)/shard_map/reshape | solution.py:147
  21.1 0.0 copy-start.1
  21.1 0.0 copy-start.2
  21.1 0.0 copy-start.3
  21.1 0.0 copy-start.4
  21.1 0.0 copy-start.5
  21.1 0.0 copy-start.6
  21.1 0.0 copy-start.7
  21.2 0.0 copy-start.8
  21.2 1.6 %copy.16 = f32[2,8,64,128]{3,2,1,0:T(8,128)S(1)} copy(f32[2,8,64,128]{2,3,1,0:T(8,128)} %bitcast.16) | data formatting | bytes 1048576 | tf_op jit(solution)/shard_map/transpose | solution.py:147
  22.8 26.7 %all-to-all-done = f32[64,2,2,8,128]{4,3,2,1,0:T(8,128)S(1)} async-done(((f32[64,2,2,8,128]{4,3,2,1,0:T(8,128)}), f32[64,2,2,8,128]{4,3,2,1,0:T(8,128)S(1)}, u32[]{:S(2)}, u32[]{:S(2)}) %all-to-all-start) | async-done | bytes 1048608 | tf_op jit(solution)/shard_map/all_to_all | solution.py:146
  49.5 0.0 copy-done.1
  49.5 0.0 copy-done.2
  49.5 0.0 copy-done.3
  49.5 0.0 copy-done.4
  49.5 0.0 copy-done.5
  49.5 0.0 copy-done.6
  49.5 0.0 copy-done.7
  49.5 0.0 copy-done.8
  49.5 5.4 %shard_map.113 = (f32[2048,128]{1,0:T(8,128)}, f32[16,128]{1,0:T(8,128)S(1)}) custom-call(f32[2048,128]{1,0:T(8,128)S(1)} %bitcast.14, f32[1024,128]{1,0:T(8,128)S(1)} %bitcast.15, bf16[256,256]{1,0:T(8,128)(2,1)S(1)} %copy-done.6, bf16[256,256]{1,0:T(8,128)(2,1)S(1)} %copy-done.5, bf16[256,256]{1,0:T(8,128)(2,1)S(1)} %copy-done.4, ...), custom_call_target="tpu_custom_call" | custom-call | flops 5368709120 | bytes 4194304 | tf_op jit(solution)/shard_map/pallas_call | solution.py:122
  55.0 6.4 %all-to-all-start.1 = ((f32[64,2,2,8,128]{4,3,2,1,0:T(8,128)}), f32[64,2,2,8,128]{4,3,2,1,0:T(8,128)S(1)}, u32[]{:S(2)}, u32[]{:S(2)}) async-start(f32[64,2,2,8,128]{4,3,2,1,0:T(8,128)} %bitcast.5), calls=%async_computation.1 | async-start | bytes 2097152 | tf_op jit(solution)/shard_map/all_to_all | solution.py:154
  61.4 0.1 reduce_sum.10
  61.5 0.1 reduce_sum.14
  61.6 10.6 %psum.7 = f32[8]{0:T(128)S(1)} all-reduce(f32[8]{0:T(128)S(1)} %reduce_sum.18), channel_id=1, replica_groups=mesh['slab'=64,'plane'=8] {'plane'}, use_global_device_ids=true, to_apply=%region_2.3 | all-reduce | flops 8 | bytes 64 | tf_op jit(solution)/shard_map/psum | solution.py:157
  72.2 0.5 broadcast_multiply_fusion
  72.7 17.4 %all-to-all-done.1 = f32[64,2,2,8,128]{4,3,2,1,0:T(8,128)S(1)} async-done(((f32[64,2,2,8,128]{4,3,2,1,0:T(8,128)}), f32[64,2,2,8,128]{4,3,2,1,0:T(8,128)S(1)}, u32[]{:S(2)}, u32[]{:S(2)}) %all-to-all-start.1) | async-done | bytes 1048608 | tf_op jit(solution)/shard_map/all_to_all | solution.py:154
  90.1 1.0 %copy_bitcast_fusion = f32[2,2,512,128]{3,2,1,0:T(8,128)} fusion(f32[64,2,2,8,128]{4,3,2,1,0:T(8,128)S(1)} %all-to-all-done.1), kind=kLoop, calls=%fused_computation | loop fusion | bytes 2097152 | tf_op jit(solution)/shard_map/reshape | solution.py:155
  (1 shorter events, 0.0 us)
Async XLA Ops:
  0.6 1.2 %copy-start = (f32[2,2,512,128]{3,2,1,0:T(8,128)S(1)}, f32[2,2,512,128]{3,2,1,0:T(8,128)}, u32[]{:S(2)}) copy-start(f32[2,2,512,128]{3,2,1,0:T(8,128)} %param.10) | copy-start | bytes 3145732
  3.0 16.7 %copy-start.9 = (f32[2,8,8192]{2,1,0:T(8,128)S(1)}, f32[2,8,8192]{2,1,0:T(8,128)}, u32[]{:S(2)}) copy-start(f32[2,8,8192]{2,1,0:T(8,128)} %param.11) | copy-start | bytes 1572868
  3.0 46.5 %all-to-all-start = ((f32[64,2,2,8,128]{4,3,2,1,0:T(8,128)}), f32[64,2,2,8,128]{4,3,2,1,0:T(8,128)S(1)}, u32[]{:S(2)}, u32[]{:S(2)}) async-start(f32[64,2,2,8,128]{4,3,2,1,0:T(8,128)} %copy_bitcast_fusion.1), calls=%async_computation | async-start | bytes 2097152 | tf_op jit(solution)/shard_map/all_to_all | solution.py:146
  21.1 28.4 %copy-start.1 = (bf16[256,256]{1,0:T(8,128)(2,1)S(1)}, bf16[256,256]{1,0:T(8,128)(2,1)}, u32[]{:S(2)}) copy-start(bf16[256,256]{1,0:T(8,128)(2,1)} %constant.26.clone.ga_lo) | copy-start | bytes 393220
  21.1 28.4 %copy-start.2 = (bf16[256,256]{1,0:T(8,128)(2,1)S(1)}, bf16[256,256]{1,0:T(8,128)(2,1)}, u32[]{:S(2)}) copy-start(bf16[256,256]{1,0:T(8,128)(2,1)} %constant.25.clone.ga_hi) | copy-start | bytes 393220
  21.1 28.4 %copy-start.3 = (bf16[256,256]{1,0:T(8,128)(2,1)S(1)}, bf16[256,256]{1,0:T(8,128)(2,1)}, u32[]{:S(2)}) copy-start(bf16[256,256]{1,0:T(8,128)(2,1)} %constant.24.clone.sp_lo) | copy-start | bytes 393220
  21.1 28.4 %copy-start.4 = (bf16[256,256]{1,0:T(8,128)(2,1)S(1)}, bf16[256,256]{1,0:T(8,128)(2,1)}, u32[]{:S(2)}) copy-start(bf16[256,256]{1,0:T(8,128)(2,1)} %constant.23.clone.sp_hi) | copy-start | bytes 393220
  21.1 28.4 %copy-start.5 = (bf16[256,256]{1,0:T(8,128)(2,1)S(1)}, bf16[256,256]{1,0:T(8,128)(2,1)}, u32[]{:S(2)}) copy-start(bf16[256,256]{1,0:T(8,128)(2,1)} %constant.22.clone.inv_ref) | copy-start | bytes 393220
  21.1 28.4 %copy-start.6 = (bf16[256,256]{1,0:T(8,128)(2,1)S(1)}, bf16[256,256]{1,0:T(8,128)(2,1)}, u32[]{:S(2)}) copy-start(bf16[256,256]{1,0:T(8,128)(2,1)} %constant.21.clone.fwd_ref) | copy-start | bytes 393220
  21.1 28.4 %copy-start.7 = (f32[64,128]{1,0:T(8,128)S(1)}, f32[64,128]{1,0:T(8,128)}, u32[]{:S(2)}) copy-start(f32[64,128]{1,0:T(8,128)} %constant.28.clone.sin_ref) | copy-start | bytes 98308
  21.2 28.4 %copy-start.8 = (f32[64,128]{1,0:T(8,128)S(1)}, f32[64,128]{1,0:T(8,128)}, u32[]{:S(2)}) copy-start(f32[64,128]{1,0:T(8,128)} %constant.27.clone.cos_ref) | copy-start | bytes 98308
  55.0 35.1 %all-to-all-start.1 = ((f32[64,2,2,8,128]{4,3,2,1,0:T(8,128)}), f32[64,2,2,8,128]{4,3,2,1,0:T(8,128)S(1)}, u32[]{:S(2)}, u32[]{:S(2)}) async-start(f32[64,2,2,8,128]{4,3,2,1,0:T(8,128)} %bitcast.5), calls=%async_computation.1 | async-start | bytes 2097152 | tf_op jit(solution)/shard_map/all_to_all | solution.py:154

commit v2 on v1

v2 whole, which is shorter than its diff:
```python
import math

import numpy as np
import ml_dtypes

import jax
import jax.numpy as jnp
from jax import lax
from jax.experimental import pallas as pl
from jax.experimental.pallas import tpu as pltpu
from jax.sharding import PartitionSpec as P


def split_constant(table):
    high = table.astype(np.float32).astype(ml_dtypes.bfloat16)
    low = (table - high.astype(np.float64)).astype(np.float32).astype(ml_dtypes.bfloat16)
    return high, low


def waves(rows, cols, size):
    product = np.outer(rows, cols) % size
    angle = 2.0 * math.pi / size * product
    return np.cos(angle), np.sin(angle)


def constant_tables(outer, inner):
    length = outer * inner
    natural, line = np.arange(outer), np.arange(inner)
    halved = np.concatenate([line[0::2], line[1::2]])
    cos_o, sin_o = waves(natural, natural, outer)
    mix = np.stack(
        [np.stack([cos_o, sin_o], axis=2), np.stack([-sin_o, cos_o], axis=2)], axis=0
    ).reshape(2 * outer, 2 * outer)
    unmix = mix.T / length
    cos_i, sin_i = waves(line, halved, inner)
    spread = np.block([[cos_i, -sin_i], [sin_i, cos_i]])
    tables = []
    for matrix in (mix, unmix):
        high, low = split_constant(matrix)
        tables.append(np.block([[high, high], [low, low]]))
    for matrix in (spread, spread.T):
        high, low = split_constant(matrix)
        tables.append(np.concatenate([high, high, low], axis=0))
    cos_t, sin_t = waves(natural, line, length)
    return tables + [cos_t.astype(np.float32), sin_t.astype(np.float32)]


def halves(value):
    high = value.astype(jnp.bfloat16)
    low = (value - high.astype(jnp.float32)).astype(jnp.bfloat16)
    return high, low


def matmul(left, right):
    return jnp.dot(left, right, preferred_element_type=jnp.float32)


def spread_rows(value, table_ref):
    high, low = halves(value)
    return matmul(jnp.concatenate([high, low, high], axis=1), table_ref[...])


def mix_lines(lines, table_ref):
    block = jnp.concatenate(lines, axis=1)
    product = matmul(table_ref[...], jnp.concatenate(halves(block), axis=0))
    rows = product.shape[0] // 2
    return product[:rows] + product[rows:]


def line_kernel(
    lines_ref, green_ref, mix_ref, unmix_ref, spread_ref, gather_ref, cos_ref, sin_ref,
    out_ref, energy_ref,
):
    outer, inner = cos_ref.shape
    rows = 2 * outer
    planes, _, per_plane, _ = green_ref.shape
    count = planes * per_plane
    pair = 2
    cos_t, sin_t = cos_ref[...], sin_ref[...]
    turned = []
    for first in range(0, count, pair):
        mixed = mix_lines(
            [lines_ref[pl.ds(first + n, rows, stride=count), :] for n in range(pair)], mix_ref
        )
        for n in range(pair):
            real = mixed[:outer, n * inner:(n + 1) * inner]
            imag = mixed[outer:, n * inner:(n + 1) * inner]
            turned.append(
                jnp.concatenate(
                    [real * cos_t + imag * sin_t, imag * cos_t - real * sin_t], axis=1
                )
            )
    spectrum = spread_rows(jnp.concatenate(turned, axis=0), spread_ref)
    weighted = []
    for line in range(count):
        green = green_ref[line // per_plane, :, line % per_plane, :].T
        green = jnp.concatenate([green[:outer], green[outer:]], axis=1)
        real = spectrum[line * outer:(line + 1) * outer, :inner]
        imag = spectrum[line * outer:(line + 1) * outer, inner:]
        green_real, green_imag = green * real, green * imag
        energy_ref[line:line + 1, :] = jnp.sum(
            green_real * real + green_imag * imag, axis=0, keepdims=True
        )
        weighted.append(jnp.concatenate([green_real, green_imag], axis=1))
    back = spread_rows(jnp.concatenate(weighted, axis=0), gather_ref)
    for first in range(0, count, pair):
        turned = []
        for line in range(first, first + pair):
            real = back[line * outer:(line + 1) * outer, :inner]
            imag = back[line * outer:(line + 1) * outer, inner:]
            turned.append(
                jnp.concatenate(
                    [real * cos_t - imag * sin_t, imag * cos_t + real * sin_t], axis=0
                )
            )
        result = mix_lines(turned, unmix_ref)
        for n in range(pair):
            out_ref[pl.ds(first + n, rows, stride=count), :] = result[:, n * inner:(n + 1) * inner]


def convolve_lines(lines, green, tables):
    vmem = pl.BlockSpec(memory_space=pltpu.VMEM)
    count = green.shape[0] * green.shape[2]
    return pl.pallas_call(
        line_kernel,
        out_shape=(
            jax.ShapeDtypeStruct(lines.shape, jnp.float32),
            jax.ShapeDtypeStruct((count, lines.shape[1]), jnp.float32),
        ),
        in_specs=[vmem] * (2 + len(tables)),
        out_specs=(vmem, vmem),
        compiler_params=pltpu.CompilerParams(vmem_limit_bytes=40 * 1024 * 1024),
        cost_estimate=pl.CostEstimate(
            flops=16 * 10 * 256**3, bytes_accessed=4 * 1024 * 1024, transcendentals=0
        ),
    )(lines, green, *tables)


def shards(density, green):
    slab_count = lax.axis_size("slab")
    parts, plane_local, lines_all, local_x = density.shape
    length = local_x * slab_count
    planes_all = plane_local * lax.axis_size("plane")
    line_local = lines_all // slab_count
    tables = [jnp.asarray(t) for t in constant_tables(slab_count, local_x)]
    tiles = density.reshape(parts, plane_local, slab_count, line_local, local_x)
    sent = jnp.transpose(tiles, (2, 0, 1, 3, 4))
    moved = lax.all_to_all(sent, "slab", split_axis=0, concat_axis=0, tiled=True)
    by_line = green.reshape(plane_local, line_local, slab_count, local_x)
    result, energy = convolve_lines(
        moved.reshape(slab_count * parts * plane_local * line_local, local_x),
        jnp.transpose(by_line, (0, 2, 1, 3)),
        tables,
    )
    result = result.reshape(slab_count, parts, plane_local, line_local, local_x)
    returned = lax.all_to_all(result, "slab", split_axis=0, concat_axis=0, tiled=True)
    potential = jnp.transpose(returned, (1, 2, 0, 3, 4)).reshape(density.shape)
    energy = jnp.sum(energy.reshape(plane_local, line_local, local_x), axis=(0, 2))
    energy = lax.psum(energy, "plane") / (length * length * planes_all)
    return (potential, energy)


def solution(mesh):
    placed = (P(None, "plane", None, "slab"), P("plane", "slab", None))
    return jax.shard_map(
        shards,
        mesh=mesh,
        in_specs=placed,
        out_specs=(P(None, "plane", None, "slab"), P("slab")),
        check_vma=False,
    )
```

time: 91.5 us -> 88.2 us (0.964)
  blocking collectives: 10.6 us -> 56.9 us
  waiting for transfers between devices: 44.1 us -> 17.4 us
  starting transfers between devices: 23.1 us -> 6.41 us
  local copies, waits for them, and re-layouts: 6.52 us -> 2.52 us
  Pallas kernels: 5.4 us -> 3.34 us
    all_to_all x0 -> x1, blocking collectives: none -> 46.3 us  [shards(): lax.all_to_all(sent, 'slab', split_axis=0, concat_axis=0, tiled=True)]
    all_to_all x1 -> x0, waiting for transfers between devices: 26.7 us -> none  [shards(): lax.all_to_all(sent, 'slab', split_axis=0, concat_axis=0, tiled=True)]
    all_to_all x1 -> x0, starting transfers between devices: 16.7 us -> none  [shards(): lax.all_to_all(sent, 'slab', split_axis=0, concat_axis=0, tiled=True)]
    pallas_call x1, Pallas kernels: 5.4 us -> 3.34 us  [convolve_lines(): pl.pallas_call(line_kernel, out_shape=(jax.ShapeDtypeStruct(lines.shape,...]
    transpose x1 -> x0, local copies, waits for them, and re-layouts: 1.62 us -> none  [shards(): jnp.swapaxes(green.reshape(plane_local, line_local, local_x, slab_count),...]
    reshape x1 -> x0, local copies, waits for them, and re-layouts: 1.39 us -> none  [shards(): green.reshape(plane_local, line_local, local_x, slab_count)]
    transpose x1, local copies, waits for them, and re-layouts: 1.11 us -> 0.13 us  [shards(): sent = jnp.transpose(tiles, (2, 0, 1, 3, 4))]
  transfers between devices with their start and end apart: 2 -> 1, of which waited for: 2 -> 1; matrix products, arithmetic and copies ran while one was open for 4% -> 1% of each run, Pallas kernels for 0% -> 0%
where the time goes in v2:
time: 88.2 us; the launch traced here: 88 us
  blocking collectives  56.9 us (65%)
  waiting for transfers between devices  17.4 us (20%)
  starting transfers between devices  6.41 us (7%)
  Pallas kernels  3.34 us (4%)
  local copies, waits for them, and re-layouts  2.52 us (3%)
    all_to_all x1, blocking collectives, shards(): lax.all_to_all(sent, 'slab', split_axis=0, concat_axis=0, tiled=True)  46.3 us
    all_to_all x1, waiting for transfers between devices, shards(): lax.all_to_all(result, 'slab', split_axis=0, concat_axis=0, tiled=True)  17.4 us
    psum x1, blocking collectives, shards(): energy = lax.psum(energy, 'plane') / (length * length * planes_all)  10.6 us
    all_to_all x1, starting transfers between devices, shards(): lax.all_to_all(result, 'slab', split_axis=0, concat_axis=0, tiled=True)  6.41 us
    pallas_call x1, Pallas kernels, convolve_lines(): pl.pallas_call(line_kernel, out_shape=(jax.ShapeDtypeStruct(lines.shape,...  3.34 us
  transfers between devices with their start and end apart: 1, of which 1 were waited for; matrix products, arithmetic and copies ran while one was open for 1% of the time, Pallas kernels for 0%

profile of v2, /device:TPU:6, one launch (start us, length us, event | category | flops | bytes accessed | tf_op | source)
XLA Modules:
  0.0 88.0 jit_solution(3412476312603526505)
XLA Ops:
  0.6 0.0 copy-start
  0.6 1.2 %copy-done = f32[2,2,512,128]{3,2,1,0:T(8,128)S(1)} copy-done((f32[2,2,512,128]{3,2,1,0:T(8,128)S(1)}, f32[2,2,512,128]{3,2,1,0:T(8,128)}, u32[]{:S(2)}) %copy-start) | copy-done | bytes 1048600
  1.9 0.1 copy_bitcast_fusion.1
  2.0 0.0 copy-start.1
  2.0 0.0 copy-start.2
  2.0 0.0 copy-start.3
  2.0 0.0 copy-start.4
  2.0 0.0 copy-start.5
  2.1 0.0 copy-start.6
  2.1 0.0 copy-start.7
  2.1 46.3 %all_to_all.10 = f32[64,2,2,8,128]{4,3,2,1,0:T(8,128)S(1)} all-to-all(f32[64,2,2,8,128]{4,3,2,1,0:T(8,128)S(1)} %copy_bitcast_fusion.1), channel_id=1, replica_groups=mesh['slab'=64,'plane'=8] {'slab'}, dimensions={0} | all-to-all | bytes 2097152 | tf_op jit(solution)/shard_map/all_to_all | solution.py:148
  48.4 0.0 copy-done.1
  48.4 0.0 copy-done.2
  48.4 0.0 copy-done.3
  48.4 0.0 copy-done.4
  48.4 0.0 copy-done.5
  48.4 0.0 copy-done.6
  48.4 0.0 copy-done.7
  48.4 3.3 %shard_map.95 = (f32[2048,128]{1,0:T(8,128)}, f32[16,128]{1,0:T(8,128)S(1)}) custom-call(f32[2048,128]{1,0:T(8,128)S(1)} %bitcast.15, f32[2,64,8,128]{3,2,1,0:T(8,128)S(1)} %bitcast.16, bf16[256,256]{1,0:T(8,128)(2,1)S(1)} %copy-done.5, bf16[256,256]{1,0:T(8,128)(2,1)S(1)} %copy-done.4, bf16[768,256]{1,0:T(8,128)(2,1)S(1)} %copy-done.3, ...), custom_call_target="tpu_custom_call" | custom-call | flops 2684354560 | bytes 4194304 | tf_op jit(solution)/shard_map/pallas_call | solution.py:124
  51.8 6.4 %all-to-all-start.1 = ((f32[64,2,2,8,128]{4,3,2,1,0:T(8,128)}), f32[64,2,2,8,128]{4,3,2,1,0:T(8,128)S(1)}, u32[]{:S(2)}, u32[]{:S(2)}) async-start(f32[64,2,2,8,128]{4,3,2,1,0:T(8,128)} %bitcast.5), calls=%async_computation.1 | async-start | bytes 2097152 | tf_op jit(solution)/shard_map/all_to_all | solution.py:156
  58.2 0.1 reduce_sum.10
  58.3 0.1 reduce_sum.14
  58.4 10.6 %psum.7 = f32[8]{0:T(128)S(1)} all-reduce(f32[8]{0:T(128)S(1)} %reduce_sum.18), channel_id=1, replica_groups=mesh['slab'=64,'plane'=8] {'plane'}, use_global_device_ids=true, to_apply=%region_2.3 | all-reduce | flops 8 | bytes 64 | tf_op jit(solution)/shard_map/psum | solution.py:159
  69.0 0.5 broadcast_multiply_fusion
  69.5 17.4 %all-to-all-done.1 = f32[64,2,2,8,128]{4,3,2,1,0:T(8,128)S(1)} async-done(((f32[64,2,2,8,128]{4,3,2,1,0:T(8,128)}), f32[64,2,2,8,128]{4,3,2,1,0:T(8,128)S(1)}, u32[]{:S(2)}, u32[]{:S(2)}) %all-to-all-start.1) | async-done | bytes 1048608 | tf_op jit(solution)/shard_map/all_to_all | solution.py:156
  86.9 1.0 %copy_bitcast_fusion = f32[2,2,512,128]{3,2,1,0:T(8,128)} fusion(f32[64,2,2,8,128]{4,3,2,1,0:T(8,128)S(1)} %all-to-all-done.1), kind=kLoop, calls=%fused_computation | loop fusion | bytes 2097152 | tf_op jit(solution)/shard_map/reshape | solution.py:157
  (1 shorter events, 0.0 us)
Async XLA Ops:
  0.6 1.2 %copy-start = (f32[2,2,512,128]{3,2,1,0:T(8,128)S(1)}, f32[2,2,512,128]{3,2,1,0:T(8,128)}, u32[]{:S(2)}) copy-start(f32[2,2,512,128]{3,2,1,0:T(8,128)} %param.8) | copy-start | bytes 3145732
  2.0 46.4 %copy-start.1 = (f32[2,8,8192]{2,1,0:T(8,128)S(1)}, f32[2,8,8192]{2,1,0:T(8,128)}, u32[]{:S(2)}) copy-start(f32[2,8,8192]{2,1,0:T(8,128)} %param.9) | copy-start | bytes 1572868
  2.0 46.4 %copy-start.2 = (bf16[768,256]{1,0:T(8,128)(2,1)S(1)}, bf16[768,256]{1,0:T(8,128)(2,1)}, u32[]{:S(2)}) copy-start(bf16[768,256]{1,0:T(8,128)(2,1)} %constant.20.clone.gather_ref) | copy-start | bytes 1179652
  2.0 46.4 %copy-start.3 = (bf16[768,256]{1,0:T(8,128)(2,1)S(1)}, bf16[768,256]{1,0:T(8,128)(2,1)}, u32[]{:S(2)}) copy-start(bf16[768,256]{1,0:T(8,128)(2,1)} %constant.19.clone.spread_ref) | copy-start | bytes 1179652
  2.0 46.4 %copy-start.4 = (bf16[256,256]{1,0:T(8,128)(2,1)S(1)}, bf16[256,256]{1,0:T(8,128)(2,1)}, u32[]{:S(2)}) copy-start(bf16[256,256]{1,0:T(8,128)(2,1)} %constant.18.clone.unmix_ref) | copy-start | bytes 393220
  2.0 46.4 %copy-start.5 = (bf16[256,256]{1,0:T(8,128)(2,1)S(1)}, bf16[256,256]{1,0:T(8,128)(2,1)}, u32[]{:S(2)}) copy-start(bf16[256,256]{1,0:T(8,128)(2,1)} %constant.17.clone.mix_ref) | copy-start | bytes 393220
  2.1 46.4 %copy-start.6 = (f32[64,128]{1,0:T(8,128)S(1)}, f32[64,128]{1,0:T(8,128)}, u32[]{:S(2)}) copy-start(f32[64,128]{1,0:T(8,128)} %constant.22.clone.sin_ref) | copy-start | bytes 98308
  2.1 46.4 %copy-start.7 = (f32[64,128]{1,0:T(8,128)S(1)}, f32[64,128]{1,0:T(8,128)}, u32[]{:S(2)}) copy-start(f32[64,128]{1,0:T(8,128)} %constant.21.clone.cos_ref) | copy-start | bytes 98308
  51.8 35.1 %all-to-all-start.1 = ((f32[64,2,2,8,128]{4,3,2,1,0:T(8,128)}), f32[64,2,2,8,128]{4,3,2,1,0:T(8,128)S(1)}, u32[]{:S(2)}, u32[]{:S(2)}) async-start(f32[64,2,2,8,128]{4,3,2,1,0:T(8,128)} %bitcast.5), calls=%async_computation.1 | async-start | bytes 2097152 | tf_op jit(solution)/shard_map/all_to_all | solution.py:156

commit v3 on v2

--- a/solution.py
+++ b/solution.py
@@ -1,3 +1,4 @@
+from functools import partial
 import math
 
 import numpy as np
@@ -23,19 +24,22 @@
     return np.cos(angle), np.sin(angle)
 
 
-def constant_tables(outer, inner):
+def constant_tables(arrival, departure, inner):
+    outer = len(arrival)
     length = outer * inner
     natural, line = np.arange(outer), np.arange(inner)
     halved = np.concatenate([line[0::2], line[1::2]])
-    cos_o, sin_o = waves(natural, natural, outer)
-    mix = np.stack(
-        [np.stack([cos_o, sin_o], axis=2), np.stack([-sin_o, cos_o], axis=2)], axis=0
-    ).reshape(2 * outer, 2 * outer)
-    unmix = mix.T / length
+    mixes = []
+    for order in (arrival, departure):
+        cos_o, sin_o = waves(natural, order, outer)
+        mix = np.stack(
+            [np.stack([cos_o, sin_o], axis=2), np.stack([-sin_o, cos_o], axis=2)], axis=0
+        )
+        mixes.append(mix.reshape(2 * outer, 2 * outer))
     cos_i, sin_i = waves(line, halved, inner)
     spread = np.block([[cos_i, -sin_i], [sin_i, cos_i]])
     tables = []
-    for matrix in (mix, unmix):
+    for matrix in (mixes[0], mixes[1].T / length):
         high, low = split_constant(matrix)
         tables.append(np.block([[high, high], [low, low]]))
     for matrix in (spread, spread.T):
@@ -137,23 +141,37 @@
 
 
 def shards(density, green):
-    slab_count = lax.axis_size("slab")
+    slab_count, plane_count = lax.axis_size("slab"), lax.axis_size("plane")
     parts, plane_local, lines_all, local_x = density.shape
     length = local_x * slab_count
-    planes_all = plane_local * lax.axis_size("plane")
+    planes_all = plane_local * plane_count
     line_local = lines_all // slab_count
-    tables = [jnp.asarray(t) for t in constant_tables(slab_count, local_x)]
+    first = slab_count - 5 * slab_count // 16
+    order = np.roll(np.arange(slab_count), -first)
+    groups = [
+        [int(slab) * plane_count + plane for slab in order] for plane in range(plane_count)
+    ]
+    exchange = partial(
+        lax.all_to_all,
+        axis_name=("slab", "plane"),
+        split_axis=0,
+        concat_axis=0,
+        axis_index_groups=groups,
+        tiled=True,
+    )
+    tables = [jnp.asarray(t) for t in constant_tables(order, order, local_x)]
     tiles = density.reshape(parts, plane_local, slab_count, line_local, local_x)
     sent = jnp.transpose(tiles, (2, 0, 1, 3, 4))
-    moved = lax.all_to_all(sent, "slab", split_axis=0, concat_axis=0, tiled=True)
+    sent = jnp.concatenate([sent[first:], sent[:first]], axis=0)
+    moved = exchange(sent)
     by_line = green.reshape(plane_local, line_local, slab_count, local_x)
     result, energy = convolve_lines(
         moved.reshape(slab_count * parts * plane_local * line_local, local_x),
         jnp.transpose(by_line, (0, 2, 1, 3)),
         tables,
     )
-    result = result.reshape(slab_count, parts, plane_local, line_local, local_x)
-    returned = lax.all_to_all(result, "slab", split_axis=0, concat_axis=0, tiled=True)
+    returned = exchange(result.reshape(sent.shape))
+    returned = jnp.concatenate([returned[slab_count - first:], returned[:slab_count - first]], axis=0)
     potential = jnp.transpose(returned, (1, 2, 0, 3, 4)).reshape(density.shape)
     energy = jnp.sum(energy.reshape(plane_local, line_local, local_x), axis=(0, 2))
     energy = lax.psum(energy, "plane") / (length * length * planes_all)

time: 88.2 us -> 85.3 us (0.967)
  starting transfers between devices: 6.41 us -> 12.4 us
  waiting for transfers between devices: 17.4 us -> 11.5 us
  blocking collectives: 56.9 us -> 53.5 us
  other arithmetic: 0.65 us -> 1.76 us
  local copies, waits for them, and re-layouts: 2.52 us -> 1.63 us
    all_to_all x1, starting transfers between devices: 6.41 us -> 12.4 us  [shards(): returned = exchange(result.reshape(sent.shape))]
    all_to_all x1, waiting for transfers between devices: 17.4 us -> 11.5 us  [shards(): returned = exchange(result.reshape(sent.shape))]
    all_to_all x1, blocking collectives: 46.3 us -> 42.9 us  [shards(): moved = exchange(sent)]
    reshape x0 -> x1, other arithmetic: none -> 1.04 us  [shards(): potential = jnp.transpose(returned, (1, 2, 0, 3, 4)).reshape(density.shape)]
    reshape x1 -> x0, local copies, waits for them, and re-layouts: 1.04 us -> none  [shards(): potential = jnp.transpose(returned, (1, 2, 0, 3, 4)).reshape(density.shape)]
where the time goes in v3:
time: 85.3 us; the launch traced here: 85 us
  blocking collectives  53.5 us (63%)
  starting transfers between devices  12.4 us (15%)
  waiting for transfers between devices  11.5 us (13%)
  Pallas kernels  3.34 us (4%)
  other arithmetic  1.76 us (2%)
  local copies, waits for them, and re-layouts  1.63 us (2%)
    all_to_all x1, blocking collectives, shards(): moved = exchange(sent)  42.9 us
    all_to_all x1, starting transfers between devices, shards(): returned = exchange(result.reshape(sent.shape))  12.4 us
    all_to_all x1, waiting for transfers between devices, shards(): returned = exchange(result.reshape(sent.shape))  11.5 us
    psum x1, blocking collectives, shards(): energy = lax.psum(energy, 'plane') / (length * length * planes_all)  10.6 us
    pallas_call x1, Pallas kernels, convolve_lines(): pl.pallas_call(line_kernel, out_shape=(jax.ShapeDtypeStruct(lines.shape,...  3.34 us
  transfers between devices with their start and end apart: 1, of which 1 were waited for; matrix products, arithmetic and copies ran while one was open for 1% of the time, Pallas kernels for 0%

profile of v3, /device:TPU:6, one launch (start us, length us, event | category | flops | bytes accessed | tf_op | source)
XLA Modules:
  0.0 85.0 jit_solution(16883527825197926879)
XLA Ops:
  0.6 0.0 copy-start
  0.6 1.2 %copy-done = f32[2,2,512,128]{3,2,1,0:T(8,128)S(1)} copy-done((f32[2,2,512,128]{3,2,1,0:T(8,128)S(1)}, f32[2,2,512,128]{3,2,1,0:T(8,128)}, u32[]{:S(2)}) %copy-start) | copy-done | bytes 1048600
  1.9 0.1 copy_bitcast_fusion.1
  2.1 0.1 pad_maximum_fusion
  2.2 0.0 copy-start.1
  2.2 0.0 copy-start.2
  2.2 0.0 copy-start.3
  2.2 0.0 copy-start.4
  2.2 0.0 copy-start.5
  2.2 0.0 copy-start.6
  2.2 0.0 copy-start.7
  2.2 42.9 %all_to_all.10 = f32[64,2,2,8,128]{4,3,2,1,0:T(8,128)S(1)} all-to-all(f32[64,2,2,8,128]{4,3,2,1,0:T(8,128)S(1)} %pad_maximum_fusion), channel_id=1, replica_groups={{352,360,368,376,384,392,400,408,416,424,432,440,448,456,464,472,480,48..., dimensions={0} | all-to-all | bytes 2097152 | tf_op jit(solution)/shard_map/all_to_all | solution.py:166
  45.2 0.0 copy-done.1
  45.2 0.0 copy-done.2
  45.2 0.0 copy-done.3
  45.2 0.0 copy-done.4
  45.2 0.0 copy-done.5
  45.2 0.0 copy-done.6
  45.2 0.0 copy-done.7
  45.2 3.3 %shard_map.95 = (f32[2048,128]{1,0:T(8,128)}, f32[16,128]{1,0:T(8,128)S(1)}) custom-call(f32[2048,128]{1,0:T(8,128)S(1)} %bitcast.15, f32[2,64,8,128]{3,2,1,0:T(8,128)S(1)} %bitcast.16, bf16[256,256]{1,0:T(8,128)(2,1)S(1)} %copy-done.5, bf16[256,256]{1,0:T(8,128)(2,1)S(1)} %copy-done.4, bf16[768,256]{1,0:T(8,128)(2,1)S(1)} %copy-done.3, ...), custom_call_target="tpu_custom_call" | custom-call | flops 2684354560 | bytes 4194304 | tf_op jit(solution)/shard_map/pallas_call | solution.py:128
  48.6 12.4 %all-to-all-start.1 = ((f32[64,2,2,8,128]{4,3,2,1,0:T(8,128)}), f32[64,2,2,8,128]{4,3,2,1,0:T(8,128)S(1)}, u32[]{:S(2)}, u32[]{:S(2)}) async-start(f32[64,2,2,8,128]{4,3,2,1,0:T(8,128)} %bitcast.5), calls=%async_computation.1 | async-start | bytes 2097152 | tf_op jit(solution)/shard_map/all_to_all | solution.py:173
  61.0 0.1 reduce_sum.10
  61.1 0.1 reduce_sum.14
  61.3 10.6 %psum.7 = f32[8]{0:T(128)S(1)} all-reduce(f32[8]{0:T(128)S(1)} %reduce_sum.18), channel_id=1, replica_groups=mesh['slab'=64,'plane'=8] {'plane'}, use_global_device_ids=true, to_apply=%region_2.3 | all-reduce | flops 8 | bytes 64 | tf_op jit(solution)/shard_map/psum | solution.py:177
  71.8 0.5 broadcast_multiply_fusion
  72.4 11.5 %all-to-all-done.1 = f32[64,2,2,8,128]{4,3,2,1,0:T(8,128)S(1)} async-done(((f32[64,2,2,8,128]{4,3,2,1,0:T(8,128)}), f32[64,2,2,8,128]{4,3,2,1,0:T(8,128)S(1)}, u32[]{:S(2)}, u32[]{:S(2)}) %all-to-all-start.1) | async-done | bytes 1048608 | tf_op jit(solution)/shard_map/all_to_all | solution.py:173
  83.9 1.0 %copy_bitcast_fusion = f32[2,2,512,128]{3,2,1,0:T(8,128)} fusion(f32[20,2,2,8,128]{4,3,2,1,0:T(8,128)S(1)} %slice.19, f32[44,2,2,8,128]{4,3,2,1,0:T(8,128)S(1)} %slice.18), kind=kLoop, calls=%fused_computation.2 | loop fusion | flops 262144 | bytes 2097152 | tf_op jit(solution)/shard_map/reshape | solution.py:175
  (5 shorter events, 0.2 us)
Async XLA Ops:
  0.6 1.2 %copy-start = (f32[2,2,512,128]{3,2,1,0:T(8,128)S(1)}, f32[2,2,512,128]{3,2,1,0:T(8,128)}, u32[]{:S(2)}) copy-start(f32[2,2,512,128]{3,2,1,0:T(8,128)} %param.8) | copy-start | bytes 3145732
  2.2 43.0 %copy-start.1 = (f32[2,8,8192]{2,1,0:T(8,128)S(1)}, f32[2,8,8192]{2,1,0:T(8,128)}, u32[]{:S(2)}) copy-start(f32[2,8,8192]{2,1,0:T(8,128)} %param.9) | copy-start | bytes 1572868
  2.2 43.0 %copy-start.2 = (bf16[768,256]{1,0:T(8,128)(2,1)S(1)}, bf16[768,256]{1,0:T(8,128)(2,1)}, u32[]{:S(2)}) copy-start(bf16[768,256]{1,0:T(8,128)(2,1)} %constant.20.clone.gather_ref) | copy-start | bytes 1179652
  2.2 43.0 %copy-start.3 = (bf16[768,256]{1,0:T(8,128)(2,1)S(1)}, bf16[768,256]{1,0:T(8,128)(2,1)}, u32[]{:S(2)}) copy-start(bf16[768,256]{1,0:T(8,128)(2,1)} %constant.19.clone.spread_ref) | copy-start | bytes 1179652
  2.2 43.0 %copy-start.4 = (bf16[256,256]{1,0:T(8,128)(2,1)S(1)}, bf16[256,256]{1,0:T(8,128)(2,1)}, u32[]{:S(2)}) copy-start(bf16[256,256]{1,0:T(8,128)(2,1)} %constant.18.clone.unmix_ref) | copy-start | bytes 393220
  2.2 43.0 %copy-start.5 = (bf16[256,256]{1,0:T(8,128)(2,1)S(1)}, bf16[256,256]{1,0:T(8,128)(2,1)}, u32[]{:S(2)}) copy-start(bf16[256,256]{1,0:T(8,128)(2,1)} %constant.17.clone.mix_ref) | copy-start | bytes 393220
  2.2 43.0 %copy-start.6 = (f32[64,128]{1,0:T(8,128)S(1)}, f32[64,128]{1,0:T(8,128)}, u32[]{:S(2)}) copy-start(f32[64,128]{1,0:T(8,128)} %constant.22.clone.sin_ref) | copy-start | bytes 98308
  2.2 43.0 %copy-start.7 = (f32[64,128]{1,0:T(8,128)S(1)}, f32[64,128]{1,0:T(8,128)}, u32[]{:S(2)}) copy-start(f32[64,128]{1,0:T(8,128)} %constant.21.clone.cos_ref) | copy-start | bytes 98308
  48.6 35.3 %all-to-all-start.1 = ((f32[64,2,2,8,128]{4,3,2,1,0:T(8,128)}), f32[64,2,2,8,128]{4,3,2,1,0:T(8,128)S(1)}, u32[]{:S(2)}, u32[]{:S(2)}) async-start(f32[64,2,2,8,128]{4,3,2,1,0:T(8,128)} %bitcast.5), calls=%async_computation.1 | async-start | bytes 2097152 | tf_op jit(solution)/shard_map/all_to_all | solution.py:173

commit v4 on v3

--- a/solution.py
+++ b/solution.py
@@ -81,45 +81,68 @@
     count = planes * per_plane
     pair = 2
     cos_t, sin_t = cos_ref[...], sin_ref[...]
-    turned = []
-    for first in range(0, count, pair):
-        mixed = mix_lines(
-            [lines_ref[pl.ds(first + n, rows, stride=count), :] for n in range(pair)], mix_ref
-        )
-        for n in range(pair):
-            real = mixed[:outer, n * inner:(n + 1) * inner]
-            imag = mixed[outer:, n * inner:(n + 1) * inner]
-            turned.append(
-                jnp.concatenate(
-                    [real * cos_t + imag * sin_t, imag * cos_t - real * sin_t], axis=1
+    def enter(first, size):
+        turned = []
+        for line in range(first, first + size, pair):
+            mixed = mix_lines(
+                [lines_ref[pl.ds(line + n, rows, stride=count), :] for n in range(pair)], mix_ref
+            )
+            for n in range(pair):
+                real = mixed[:outer, n * inner:(n + 1) * inner]
+                imag = mixed[outer:, n * inner:(n + 1) * inner]
+                turned.append(
+                    jnp.concatenate(
+                        [real * cos_t + imag * sin_t, imag * cos_t - real * sin_t], axis=1
+                    )
                 )
+        return jnp.concatenate(turned, axis=0)
+
+    def weigh(first, size, spectrum):
+        weighted = []
+        for n in range(size):
+            line = first + n
+            green = green_ref[line // per_plane, :, line % per_plane, :].T
+            green = jnp.concatenate([green[:outer], green[outer:]], axis=1)
+            real = spectrum[n * outer:(n + 1) * outer, :inner]
+            imag = spectrum[n * outer:(n + 1) * outer, inner:]
+            green_real, green_imag = green * real, green * imag
+            energy_ref[line:line + 1, :] = jnp.sum(
+                green_real * real + green_imag * imag, axis=0, keepdims=True
             )
-    spectrum = spread_rows(jnp.concatenate(turned, axis=0), spread_ref)
-    weighted = []
-    for line in range(count):
-        green = green_ref[line // per_plane, :, line % per_plane, :].T
-        green = jnp.concatenate([green[:outer], green[outer:]], axis=1)
-        real = spectrum[line * outer:(line + 1) * outer, :inner]
-        imag = spectrum[line * outer:(line + 1) * outer, inner:]
-        green_real, green_imag = green * real, green * imag
-        energy_ref[line:line + 1, :] = jnp.sum(
-            green_real * real + green_imag * imag, axis=0, keepdims=True
-        )
-        weighted.append(jnp.concatenate([green_real, green_imag], axis=1))
-    back = spread_rows(jnp.concatenate(weighted, axis=0), gather_ref)
-    for first in range(0, count, pair):
-        turned = []
-        for line in range(first, first + pair):
-            real = back[line * outer:(line + 1) * outer, :inner]
-            imag = back[line * outer:(line + 1) * outer, inner:]
-            turned.append(
-                jnp.concatenate(
-                    [real * cos_t - imag * sin_t, imag * cos_t + real * sin_t], axis=0
+            weighted.append(jnp.concatenate([green_real, green_imag], axis=1))
+        return jnp.concatenate(weighted, axis=0)
+
+    def leave(first, size, back):
+        for start in range(0, size, pair):
+            turned = []
+            for n in range(start, start + pair):
+                real = back[n * outer:(n + 1) * outer, :inner]
+                imag = back[n * outer:(n + 1) * outer, inner:]
+                turned.append(
+                    jnp.concatenate(
+                        [real * cos_t - imag * sin_t, imag * cos_t + real * sin_t], axis=0
+                    )
                 )
-            )
-        result = mix_lines(turned, unmix_ref)
-        for n in range(pair):
-            out_ref[pl.ds(first + n, rows, stride=count), :] = result[:, n * inner:(n + 1) * inner]
+            result = mix_lines(turned, unmix_ref)
+            for n in range(pair):
+                line = first + start + n
+                out_ref[pl.ds(line, rows, stride=count), :] = result[:, n * inner:(n + 1) * inner]
+
+    groups = 2
+    size = count // groups
+    state = {}
+    stages = [
+        lambda g: enter(g * size, size),
+        lambda g: spread_rows(state[g], spread_ref),
+        lambda g: weigh(g * size, size, state[g]),
+        lambda g: spread_rows(state[g], gather_ref),
+        lambda g: leave(g * size, size, state[g]),
+    ]
+    for wave in range(groups + len(stages) - 1):
+        for stage, run in enumerate(stages):
+            group = wave - stage
+            if 0 <= group < groups:
+                state[group] = run(group)
 
 
 def convolve_lines(lines, green, tables):

time: 85.3 us -> 85 us (level)
  no operation moved by 1% of the time
where the time goes in v4:
time: 85 us; the launch traced here: 84.6 us
  blocking collectives  53.5 us (63%)
  starting transfers between devices  12.4 us (15%)
  waiting for transfers between devices  11.5 us (14%)
  Pallas kernels  3.02 us (4%)
  other arithmetic  1.76 us (2%)
  local copies, waits for them, and re-layouts  1.63 us (2%)
    all_to_all x1, blocking collectives, shards(): moved = exchange(sent)  42.9 us
    all_to_all x1, starting transfers between devices, shards(): returned = exchange(result.reshape(sent.shape))  12.4 us
    all_to_all x1, waiting for transfers between devices, shards(): returned = exchange(result.reshape(sent.shape))  11.5 us
    psum x1, blocking collectives, shards(): energy = lax.psum(energy, 'plane') / (length * length * planes_all)  10.6 us
    pallas_call x1, Pallas kernels, convolve_lines(): pl.pallas_call(line_kernel, out_shape=(jax.ShapeDtypeStruct(lines.shape,...  3.02 us
  transfers between devices with their start and end apart: 1, of which 1 were waited for; matrix products, arithmetic and copies ran while one was open for 1% of the time, Pallas kernels for 0%

profile of v4, /device:TPU:6, one launch (start us, length us, event | category | flops | bytes accessed | tf_op | source)
XLA Modules:
  0.0 84.6 jit_solution(5412894414881886657)
XLA Ops:
  0.6 0.0 copy-start
  0.6 1.2 %copy-done = f32[2,2,512,128]{3,2,1,0:T(8,128)S(1)} copy-done((f32[2,2,512,128]{3,2,1,0:T(8,128)S(1)}, f32[2,2,512,128]{3,2,1,0:T(8,128)}, u32[]{:S(2)}) %copy-start) | copy-done | bytes 1048600
  1.9 0.1 copy_bitcast_fusion.1
  2.1 0.1 pad_maximum_fusion
  2.2 0.0 copy-start.1
  2.2 0.0 copy-start.2
  2.2 0.0 copy-start.3
  2.2 0.0 copy-start.4
  2.2 0.0 copy-start.5
  2.2 0.0 copy-start.6
  2.2 0.0 copy-start.7
  2.2 42.9 %all_to_all.10 = f32[64,2,2,8,128]{4,3,2,1,0:T(8,128)S(1)} all-to-all(f32[64,2,2,8,128]{4,3,2,1,0:T(8,128)S(1)} %pad_maximum_fusion), channel_id=1, replica_groups={{352,360,368,376,384,392,400,408,416,424,432,440,448,456,464,472,480,48..., dimensions={0} | all-to-all | bytes 2097152 | tf_op jit(solution)/shard_map/all_to_all | solution.py:189
  45.2 0.0 copy-done.1
  45.2 0.0 copy-done.2
  45.2 0.0 copy-done.3
  45.2 0.0 copy-done.4
  45.2 0.0 copy-done.5
  45.2 0.0 copy-done.6
  45.2 0.0 copy-done.7
  45.2 3.0 %shard_map.95 = (f32[2048,128]{1,0:T(8,128)}, f32[16,128]{1,0:T(8,128)S(1)}) custom-call(f32[2048,128]{1,0:T(8,128)S(1)} %bitcast.15, f32[2,64,8,128]{3,2,1,0:T(8,128)S(1)} %bitcast.16, bf16[256,256]{1,0:T(8,128)(2,1)S(1)} %copy-done.5, bf16[256,256]{1,0:T(8,128)(2,1)S(1)} %copy-done.4, bf16[768,256]{1,0:T(8,128)(2,1)S(1)} %copy-done.3, ...), custom_call_target="tpu_custom_call" | custom-call | flops 2684354560 | bytes 4194304 | tf_op jit(solution)/shard_map/pallas_call | solution.py:151
  48.3 12.4 %all-to-all-start.1 = ((f32[64,2,2,8,128]{4,3,2,1,0:T(8,128)}), f32[64,2,2,8,128]{4,3,2,1,0:T(8,128)S(1)}, u32[]{:S(2)}, u32[]{:S(2)}) async-start(f32[64,2,2,8,128]{4,3,2,1,0:T(8,128)} %bitcast.5), calls=%async_computation.1 | async-start | bytes 2097152 | tf_op jit(solution)/shard_map/all_to_all | solution.py:196
  60.7 0.1 reduce_sum.10
  60.8 0.1 reduce_sum.14
  60.9 10.6 %psum.7 = f32[8]{0:T(128)S(1)} all-reduce(f32[8]{0:T(128)S(1)} %reduce_sum.18), channel_id=1, replica_groups=mesh['slab'=64,'plane'=8] {'plane'}, use_global_device_ids=true, to_apply=%region_2.3 | all-reduce | flops 8 | bytes 64 | tf_op jit(solution)/shard_map/psum | solution.py:200
  71.5 0.5 broadcast_multiply_fusion
  72.0 11.5 %all-to-all-done.1 = f32[64,2,2,8,128]{4,3,2,1,0:T(8,128)S(1)} async-done(((f32[64,2,2,8,128]{4,3,2,1,0:T(8,128)}), f32[64,2,2,8,128]{4,3,2,1,0:T(8,128)S(1)}, u32[]{:S(2)}, u32[]{:S(2)}) %all-to-all-start.1) | async-done | bytes 1048608 | tf_op jit(solution)/shard_map/all_to_all | solution.py:196
  83.6 1.0 %copy_bitcast_fusion = f32[2,2,512,128]{3,2,1,0:T(8,128)} fusion(f32[20,2,2,8,128]{4,3,2,1,0:T(8,128)S(1)} %slice.19, f32[44,2,2,8,128]{4,3,2,1,0:T(8,128)S(1)} %slice.18), kind=kLoop, calls=%fused_computation.2 | loop fusion | flops 262144 | bytes 2097152 | tf_op jit(solution)/shard_map/reshape | solution.py:198
  (5 shorter events, 0.2 us)
Async XLA Ops:
  0.6 1.2 %copy-start = (f32[2,2,512,128]{3,2,1,0:T(8,128)S(1)}, f32[2,2,512,128]{3,2,1,0:T(8,128)}, u32[]{:S(2)}) copy-start(f32[2,2,512,128]{3,2,1,0:T(8,128)} %param.8) | copy-start | bytes 3145732
  2.2 43.0 %copy-start.1 = (f32[2,8,8192]{2,1,0:T(8,128)S(1)}, f32[2,8,8192]{2,1,0:T(8,128)}, u32[]{:S(2)}) copy-start(f32[2,8,8192]{2,1,0:T(8,128)} %param.9) | copy-start | bytes 1572868
  2.2 43.0 %copy-start.2 = (bf16[768,256]{1,0:T(8,128)(2,1)S(1)}, bf16[768,256]{1,0:T(8,128)(2,1)}, u32[]{:S(2)}) copy-start(bf16[768,256]{1,0:T(8,128)(2,1)} %constant.20.clone.gather_ref) | copy-start | bytes 1179652
  2.2 43.0 %copy-start.3 = (bf16[768,256]{1,0:T(8,128)(2,1)S(1)}, bf16[768,256]{1,0:T(8,128)(2,1)}, u32[]{:S(2)}) copy-start(bf16[768,256]{1,0:T(8,128)(2,1)} %constant.19.clone.spread_ref) | copy-start | bytes 1179652
  2.2 43.0 %copy-start.4 = (bf16[256,256]{1,0:T(8,128)(2,1)S(1)}, bf16[256,256]{1,0:T(8,128)(2,1)}, u32[]{:S(2)}) copy-start(bf16[256,256]{1,0:T(8,128)(2,1)} %constant.18.clone.unmix_ref) | copy-start | bytes 393220
  2.2 43.0 %copy-start.5 = (bf16[256,256]{1,0:T(8,128)(2,1)S(1)}, bf16[256,256]{1,0:T(8,128)(2,1)}, u32[]{:S(2)}) copy-start(bf16[256,256]{1,0:T(8,128)(2,1)} %constant.17.clone.mix_ref) | copy-start | bytes 393220
  2.2 43.0 %copy-start.6 = (f32[64,128]{1,0:T(8,128)S(1)}, f32[64,128]{1,0:T(8,128)}, u32[]{:S(2)}) copy-start(f32[64,128]{1,0:T(8,128)} %constant.22.clone.sin_ref) | copy-start | bytes 98308
  2.2 43.0 %copy-start.7 = (f32[64,128]{1,0:T(8,128)S(1)}, f32[64,128]{1,0:T(8,128)}, u32[]{:S(2)}) copy-start(f32[64,128]{1,0:T(8,128)} %constant.21.clone.cos_ref) | copy-start | bytes 98308
  48.3 35.3 %all-to-all-start.1 = ((f32[64,2,2,8,128]{4,3,2,1,0:T(8,128)}), f32[64,2,2,8,128]{4,3,2,1,0:T(8,128)S(1)}, u32[]{:S(2)}, u32[]{:S(2)}) async-start(f32[64,2,2,8,128]{4,3,2,1,0:T(8,128)} %bitcast.5), calls=%async_computation.1 | async-start | bytes 2097152 | tf_op jit(solution)/shard_map/all_to_all | solution.py:196

commit v5 on v4

--- a/solution.py
+++ b/solution.py
@@ -81,6 +81,7 @@
     count = planes * per_plane
     pair = 2
     cos_t, sin_t = cos_ref[...], sin_ref[...]
+
     def enter(first, size):
         turned = []
         for line in range(first, first + size, pair):
@@ -161,6 +162,53 @@
             flops=16 * 10 * 256**3, bytes_accessed=4 * 1024 * 1024, transcendentals=0
         ),
     )(lines, green, *tables)
+
+
+def pack_messages(tiles, order):
+    def kernel(tiles_ref, sent_ref):
+        for rank, slab in enumerate(order):
+            sent_ref[rank] = tiles_ref[int(slab)]
+
+    vmem = pl.BlockSpec(memory_space=pltpu.VMEM)
+    return pl.pallas_call(
+        kernel,
+        out_shape=jax.ShapeDtypeStruct(tiles.shape, tiles.dtype),
+        in_specs=[vmem],
+        out_specs=vmem,
+        compiler_params=pltpu.CompilerParams(vmem_limit_bytes=8 * 1024 * 1024),
+    )(tiles)
+
+
+def unpack_messages(returned, order):
+    slabs, parts, planes, *tile = returned.shape
+    shape = (parts, planes, slabs, *tile)
+
+    def kernel(returned_ref, out_ref, staged, sems):
+        copies = []
+        for part in range(parts):
+            for plane in range(planes):
+                for rank, slab in enumerate(order):
+                    staged[part, plane, int(slab)] = returned_ref[rank, part, plane]
+                copies.append(
+                    pltpu.make_async_copy(
+                        staged.at[part, plane], out_ref.at[part, plane], sems.at[part, plane]
+                    )
+                )
+                copies[-1].start()
+        for copy in copies:
+            copy.wait()
+
+    return pl.pallas_call(
+        kernel,
+        out_shape=jax.ShapeDtypeStruct(shape, returned.dtype),
+        in_specs=[pl.BlockSpec(memory_space=pltpu.VMEM)],
+        out_specs=pl.BlockSpec(memory_space=pl.ANY),
+        scratch_shapes=[
+            pltpu.VMEM(shape, returned.dtype),
+            pltpu.SemaphoreType.DMA((parts, planes)),
+        ],
+        compiler_params=pltpu.CompilerParams(vmem_limit_bytes=8 * 1024 * 1024),
+    )(returned)
 
 
 def shards(density, green):
@@ -185,7 +233,7 @@
     tables = [jnp.asarray(t) for t in constant_tables(order, order, local_x)]
     tiles = density.reshape(parts, plane_local, slab_count, line_local, local_x)
     sent = jnp.transpose(tiles, (2, 0, 1, 3, 4))
-    sent = jnp.concatenate([sent[first:], sent[:first]], axis=0)
+    sent = pack_messages(sent, order)
     moved = exchange(sent)
     by_line = green.reshape(plane_local, line_local, slab_count, local_x)
     result, energy = convolve_lines(
@@ -194,8 +242,7 @@
         tables,
     )
     returned = exchange(result.reshape(sent.shape))
-    returned = jnp.concatenate([returned[slab_count - first:], returned[:slab_count - first]], axis=0)
-    potential = jnp.transpose(returned, (1, 2, 0, 3, 4)).reshape(density.shape)
+    potential = unpack_messages(returned, order).reshape(density.shape)
     energy = jnp.sum(energy.reshape(plane_local, line_local, local_x), axis=(0, 2))
     energy = lax.psum(energy, "plane") / (length * length * planes_all)
     return (potential, energy)

time: 85 us -> 84.8 us (level)
  other arithmetic: 1.76 us -> 0.65 us
  Pallas kernels: 3.02 us -> 4.12 us
    pallas_call x0 -> x2, Pallas kernels: none -> 1.1 us  [the longest x1 1.03 us: unpack_messages(): pl.pallas_call(kernel, out_shape=jax.ShapeDtypeStruct(shape, returned.dty...]
    reshape x1 -> x0, other arithmetic: 1.04 us -> none  [shards(): potential = jnp.transpose(returned, (1, 2, 0, 3, 4)).reshape(density.shape)]
where the time goes in v5:
time: 84.8 us; the launch traced here: 84.5 us
  blocking collectives  53.5 us (63%)
  starting transfers between devices  12.4 us (15%)
  waiting for transfers between devices  11.5 us (14%)
  Pallas kernels  4.12 us (5%)
  local copies, waits for them, and re-layouts  1.48 us (2%)
    all_to_all x1, blocking collectives, shards(): moved = exchange(sent)  42.9 us
    all_to_all x1, starting transfers between devices, shards(): returned = exchange(result.reshape(sent.shape))  12.4 us
    all_to_all x1, waiting for transfers between devices, shards(): returned = exchange(result.reshape(sent.shape))  11.5 us
    psum x1, blocking collectives, shards(): energy = lax.psum(energy, 'plane') / (length * length * planes_all)  10.6 us
    pallas_call x1, Pallas kernels, convolve_lines(): pl.pallas_call(line_kernel, out_shape=(jax.ShapeDtypeStruct(lines.shape,...  3.02 us
  transfers between devices with their start and end apart: 1, of which 1 were waited for; matrix products, arithmetic and copies ran while one was open for 1% of the time, Pallas kernels for 0%

profile of v5, /device:TPU:6, one launch (start us, length us, event | category | flops | bytes accessed | tf_op | source)
XLA Modules:
  0.0 84.5 jit_solution(11196894790195631509)
XLA Ops:
  0.6 0.0 copy-start
  0.6 1.2 %copy-done = f32[2,2,512,128]{3,2,1,0:T(8,128)S(1)} copy-done((f32[2,2,512,128]{3,2,1,0:T(8,128)S(1)}, f32[2,2,512,128]{3,2,1,0:T(8,128)}, u32[]{:S(2)}) %copy-start) | copy-done | bytes 1048600
  1.9 0.1 copy_bitcast_fusion.tiles_ref
  2.0 0.1 shard_map.95
  2.1 0.0 copy-start.1
  2.1 0.0 copy-start.2
  2.1 0.0 copy-start.3
  2.1 0.0 copy-start.4
  2.1 0.0 copy-start.5
  2.1 0.0 copy-start.6
  2.1 0.0 copy-start.7
  2.2 42.9 %all_to_all.10 = f32[64,2,2,8,128]{4,3,2,1,0:T(8,128)S(1)} all-to-all(f32[64,2,2,8,128]{4,3,2,1,0:T(8,128)S(1)} %shard_map.95), channel_id=1, replica_groups={{352,360,368,376,384,392,400,408,416,424,432,440,448,456,464,472,480,48..., dimensions={0} | all-to-all | bytes 2097152 | tf_op jit(solution)/shard_map/all_to_all | solution.py:237
  45.1 0.0 copy-done.1
  45.1 0.0 copy-done.2
  45.1 0.0 copy-done.3
  45.1 0.0 copy-done.4
  45.1 0.0 copy-done.5
  45.1 0.0 copy-done.6
  45.1 0.0 copy-done.7
  45.2 3.0 %shard_map.96 = (f32[2048,128]{1,0:T(8,128)}, f32[16,128]{1,0:T(8,128)S(1)}) custom-call(f32[2048,128]{1,0:T(8,128)S(1)} %bitcast.11, f32[2,64,8,128]{3,2,1,0:T(8,128)S(1)} %bitcast.12, bf16[256,256]{1,0:T(8,128)(2,1)S(1)} %copy-done.5, bf16[256,256]{1,0:T(8,128)(2,1)S(1)} %copy-done.4, bf16[768,256]{1,0:T(8,128)(2,1)S(1)} %copy-done.3, ...), custom_call_target="tpu_custom_call" | custom-call | flops 2684354560 | bytes 4194304 | tf_op jit(solution)/shard_map/pallas_call | solution.py:152
  48.2 12.4 %all-to-all-start.1 = ((f32[64,2,2,8,128]{4,3,2,1,0:T(8,128)}), f32[64,2,2,8,128]{4,3,2,1,0:T(8,128)S(1)}, u32[]{:S(2)}, u32[]{:S(2)}) async-start(f32[64,2,2,8,128]{4,3,2,1,0:T(8,128)} %bitcast.5), calls=%async_computation.1 | async-start | bytes 2097152 | tf_op jit(solution)/shard_map/all_to_all | solution.py:244
  60.6 0.1 reduce_sum.10
  60.7 0.1 reduce_sum.14
  60.8 10.6 %psum.7 = f32[8]{0:T(128)S(1)} all-reduce(f32[8]{0:T(128)S(1)} %reduce_sum.18), channel_id=1, replica_groups=mesh['slab'=64,'plane'=8] {'plane'}, use_global_device_ids=true, to_apply=%region_2.3 | all-reduce | flops 8 | bytes 64 | tf_op jit(solution)/shard_map/psum | solution.py:247
  71.4 0.5 broadcast_multiply_fusion
  72.0 11.5 %all-to-all-done.1.returned_ref = f32[64,2,2,8,128]{4,3,2,1,0:T(8,128)S(1)} async-done(((f32[64,2,2,8,128]{4,3,2,1,0:T(8,128)}), f32[64,2,2,8,128]{4,3,2,1,0:T(8,128)S(1)}, u32[]{:S(2)}, u32[]{:S(2)}) %all-to-all-start.1) | async-done | bytes 1048608 | tf_op jit(solution)/shard_map/all_to_all | solution.py:244
  83.4 1.0 %shard_map.97 = f32[2,2,64,8,128]{4,3,2,1,0:T(8,128)} custom-call(f32[64,2,2,8,128]{4,3,2,1,0:T(8,128)S(1)} %all-to-all-done.1.returned_ref), custom_call_target="tpu_custom_call" | custom-call | tf_op jit(solution)/shard_map/pallas_call | solution.py:201
  (1 shorter events, 0.0 us)
Async XLA Ops:
  0.6 1.2 %copy-start = (f32[2,2,512,128]{3,2,1,0:T(8,128)S(1)}, f32[2,2,512,128]{3,2,1,0:T(8,128)}, u32[]{:S(2)}) copy-start(f32[2,2,512,128]{3,2,1,0:T(8,128)} %param.8) | copy-start | bytes 3145732
  2.1 43.0 %copy-start.1 = (f32[2,8,8192]{2,1,0:T(8,128)S(1)}, f32[2,8,8192]{2,1,0:T(8,128)}, u32[]{:S(2)}) copy-start(f32[2,8,8192]{2,1,0:T(8,128)} %param.9) | copy-start | bytes 1572868
  2.1 43.0 %copy-start.2 = (bf16[768,256]{1,0:T(8,128)(2,1)S(1)}, bf16[768,256]{1,0:T(8,128)(2,1)}, u32[]{:S(2)}) copy-start(bf16[768,256]{1,0:T(8,128)(2,1)} %constant.20.clone.gather_ref) | copy-start | bytes 1179652
  2.1 43.0 %copy-start.3 = (bf16[768,256]{1,0:T(8,128)(2,1)S(1)}, bf16[768,256]{1,0:T(8,128)(2,1)}, u32[]{:S(2)}) copy-start(bf16[768,256]{1,0:T(8,128)(2,1)} %constant.19.clone.spread_ref) | copy-start | bytes 1179652
  2.1 43.0 %copy-start.4 = (bf16[256,256]{1,0:T(8,128)(2,1)S(1)}, bf16[256,256]{1,0:T(8,128)(2,1)}, u32[]{:S(2)}) copy-start(bf16[256,256]{1,0:T(8,128)(2,1)} %constant.18.clone.unmix_ref) | copy-start | bytes 393220
  2.1 43.0 %copy-start.5 = (bf16[256,256]{1,0:T(8,128)(2,1)S(1)}, bf16[256,256]{1,0:T(8,128)(2,1)}, u32[]{:S(2)}) copy-start(bf16[256,256]{1,0:T(8,128)(2,1)} %constant.17.clone.mix_ref) | copy-start | bytes 393220
  2.1 43.0 %copy-start.6 = (f32[64,128]{1,0:T(8,128)S(1)}, f32[64,128]{1,0:T(8,128)}, u32[]{:S(2)}) copy-start(f32[64,128]{1,0:T(8,128)} %constant.22.clone.sin_ref) | copy-start | bytes 98308
  2.1 43.0 %copy-start.7 = (f32[64,128]{1,0:T(8,128)S(1)}, f32[64,128]{1,0:T(8,128)}, u32[]{:S(2)}) copy-start(f32[64,128]{1,0:T(8,128)} %constant.21.clone.cos_ref) | copy-start | bytes 98308
  48.2 35.3 %all-to-all-start.1 = ((f32[64,2,2,8,128]{4,3,2,1,0:T(8,128)}), f32[64,2,2,8,128]{4,3,2,1,0:T(8,128)S(1)}, u32[]{:S(2)}, u32[]{:S(2)}) async-start(f32[64,2,2,8,128]{4,3,2,1,0:T(8,128)} %bitcast.5), calls=%async_computation.1 | async-start | bytes 2097152 | tf_op jit(solution)/shard_map/all_to_all | solution.py:244

commit v6 on v5

--- a/solution.py
+++ b/solution.py
@@ -79,7 +79,7 @@
     rows = 2 * outer
     planes, _, per_plane, _ = green_ref.shape
     count = planes * per_plane
-    pair = 2
+    pair = 8
     cos_t, sin_t = cos_ref[...], sin_ref[...]
 
     def enter(first, size):

time: 84.8 us -> 84.8 us (level)
  no operation moved by 1% of the time
where the time goes in v6:
time: 84.8 us; the launch traced here: 84.5 us
  blocking collectives  53.5 us (63%)
  starting transfers between devices  12.4 us (15%)
  waiting for transfers between devices  11.5 us (14%)
  Pallas kernels  4.12 us (5%)
  local copies, waits for them, and re-layouts  1.48 us (2%)
    all_to_all x1, blocking collectives, shards(): moved = exchange(sent)  42.9 us
    all_to_all x1, starting transfers between devices, shards(): returned = exchange(result.reshape(sent.shape))  12.4 us
    all_to_all x1, waiting for transfers between devices, shards(): returned = exchange(result.reshape(sent.shape))  11.5 us
    psum x1, blocking collectives, shards(): energy = lax.psum(energy, 'plane') / (length * length * planes_all)  10.6 us
    pallas_call x1, Pallas kernels, convolve_lines(): pl.pallas_call(line_kernel, out_shape=(jax.ShapeDtypeStruct(lines.shape,...  3.02 us
  transfers between devices with their start and end apart: 1, of which 1 were waited for; matrix products, arithmetic and copies ran while one was open for 1% of the time, Pallas kernels for 0%

profile of v6, /device:TPU:6, one launch (start us, length us, event | category | flops | bytes accessed | tf_op | source)
XLA Modules:
  0.0 84.5 jit_solution(11075606209439805344)
XLA Ops:
  0.6 0.0 copy-start
  0.6 1.2 %copy-done = f32[2,2,512,128]{3,2,1,0:T(8,128)S(1)} copy-done((f32[2,2,512,128]{3,2,1,0:T(8,128)S(1)}, f32[2,2,512,128]{3,2,1,0:T(8,128)}, u32[]{:S(2)}) %copy-start) | copy-done | bytes 1048600
  1.9 0.1 copy_bitcast_fusion.tiles_ref
  2.0 0.1 shard_map.95
  2.1 0.0 copy-start.1
  2.1 0.0 copy-start.2
  2.1 0.0 copy-start.3
  2.1 0.0 copy-start.4
  2.1 0.0 copy-start.5
  2.1 0.0 copy-start.6
  2.1 0.0 copy-start.7
  2.2 42.9 %all_to_all.10 = f32[64,2,2,8,128]{4,3,2,1,0:T(8,128)S(1)} all-to-all(f32[64,2,2,8,128]{4,3,2,1,0:T(8,128)S(1)} %shard_map.95), channel_id=1, replica_groups={{352,360,368,376,384,392,400,408,416,424,432,440,448,456,464,472,480,48..., dimensions={0} | all-to-all | bytes 2097152 | tf_op jit(solution)/shard_map/all_to_all | solution.py:237
  45.1 0.0 copy-done.1
  45.1 0.0 copy-done.2
  45.1 0.0 copy-done.3
  45.1 0.0 copy-done.4
  45.1 0.0 copy-done.5
  45.1 0.0 copy-done.6
  45.1 0.0 copy-done.7
  45.2 3.0 %shard_map.96 = (f32[2048,128]{1,0:T(8,128)}, f32[16,128]{1,0:T(8,128)S(1)}) custom-call(f32[2048,128]{1,0:T(8,128)S(1)} %bitcast.11, f32[2,64,8,128]{3,2,1,0:T(8,128)S(1)} %bitcast.12, bf16[256,256]{1,0:T(8,128)(2,1)S(1)} %copy-done.5, bf16[256,256]{1,0:T(8,128)(2,1)S(1)} %copy-done.4, bf16[768,256]{1,0:T(8,128)(2,1)S(1)} %copy-done.3, ...), custom_call_target="tpu_custom_call" | custom-call | flops 2684354560 | bytes 4194304 | tf_op jit(solution)/shard_map/pallas_call | solution.py:152
  48.2 12.4 %all-to-all-start.1 = ((f32[64,2,2,8,128]{4,3,2,1,0:T(8,128)}), f32[64,2,2,8,128]{4,3,2,1,0:T(8,128)S(1)}, u32[]{:S(2)}, u32[]{:S(2)}) async-start(f32[64,2,2,8,128]{4,3,2,1,0:T(8,128)} %bitcast.5), calls=%async_computation.1 | async-start | bytes 2097152 | tf_op jit(solution)/shard_map/all_to_all | solution.py:244
  60.6 0.1 reduce_sum.10
  60.7 0.1 reduce_sum.14
  60.8 10.6 %psum.7 = f32[8]{0:T(128)S(1)} all-reduce(f32[8]{0:T(128)S(1)} %reduce_sum.18), channel_id=1, replica_groups=mesh['slab'=64,'plane'=8] {'plane'}, use_global_device_ids=true, to_apply=%region_2.3 | all-reduce | flops 8 | bytes 64 | tf_op jit(solution)/shard_map/psum | solution.py:247
  71.4 0.5 broadcast_multiply_fusion
  71.9 11.5 %all-to-all-done.1.returned_ref = f32[64,2,2,8,128]{4,3,2,1,0:T(8,128)S(1)} async-done(((f32[64,2,2,8,128]{4,3,2,1,0:T(8,128)}), f32[64,2,2,8,128]{4,3,2,1,0:T(8,128)S(1)}, u32[]{:S(2)}, u32[]{:S(2)}) %all-to-all-start.1) | async-done | bytes 1048608 | tf_op jit(solution)/shard_map/all_to_all | solution.py:244
  83.4 1.0 %shard_map.97 = f32[2,2,64,8,128]{4,3,2,1,0:T(8,128)} custom-call(f32[64,2,2,8,128]{4,3,2,1,0:T(8,128)S(1)} %all-to-all-done.1.returned_ref), custom_call_target="tpu_custom_call" | custom-call | tf_op jit(solution)/shard_map/pallas_call | solution.py:201
  (1 shorter events, 0.0 us)
Async XLA Ops:
  0.6 1.2 %copy-start = (f32[2,2,512,128]{3,2,1,0:T(8,128)S(1)}, f32[2,2,512,128]{3,2,1,0:T(8,128)}, u32[]{:S(2)}) copy-start(f32[2,2,512,128]{3,2,1,0:T(8,128)} %param.8) | copy-start | bytes 3145732
  2.1 43.0 %copy-start.1 = (f32[2,8,8192]{2,1,0:T(8,128)S(1)}, f32[2,8,8192]{2,1,0:T(8,128)}, u32[]{:S(2)}) copy-start(f32[2,8,8192]{2,1,0:T(8,128)} %param.9) | copy-start | bytes 1572868
  2.1 43.0 %copy-start.2 = (bf16[768,256]{1,0:T(8,128)(2,1)S(1)}, bf16[768,256]{1,0:T(8,128)(2,1)}, u32[]{:S(2)}) copy-start(bf16[768,256]{1,0:T(8,128)(2,1)} %constant.20.clone.gather_ref) | copy-start | bytes 1179652
  2.1 43.0 %copy-start.3 = (bf16[768,256]{1,0:T(8,128)(2,1)S(1)}, bf16[768,256]{1,0:T(8,128)(2,1)}, u32[]{:S(2)}) copy-start(bf16[768,256]{1,0:T(8,128)(2,1)} %constant.19.clone.spread_ref) | copy-start | bytes 1179652
  2.1 43.0 %copy-start.4 = (bf16[256,256]{1,0:T(8,128)(2,1)S(1)}, bf16[256,256]{1,0:T(8,128)(2,1)}, u32[]{:S(2)}) copy-start(bf16[256,256]{1,0:T(8,128)(2,1)} %constant.18.clone.unmix_ref) | copy-start | bytes 393220
  2.1 43.0 %copy-start.5 = (bf16[256,256]{1,0:T(8,128)(2,1)S(1)}, bf16[256,256]{1,0:T(8,128)(2,1)}, u32[]{:S(2)}) copy-start(bf16[256,256]{1,0:T(8,128)(2,1)} %constant.17.clone.mix_ref) | copy-start | bytes 393220
  2.1 43.0 %copy-start.6 = (f32[64,128]{1,0:T(8,128)S(1)}, f32[64,128]{1,0:T(8,128)}, u32[]{:S(2)}) copy-start(f32[64,128]{1,0:T(8,128)} %constant.22.clone.sin_ref) | copy-start | bytes 98308
  2.1 43.0 %copy-start.7 = (f32[64,128]{1,0:T(8,128)S(1)}, f32[64,128]{1,0:T(8,128)}, u32[]{:S(2)}) copy-start(f32[64,128]{1,0:T(8,128)} %constant.21.clone.cos_ref) | copy-start | bytes 98308
  48.2 35.3 %all-to-all-start.1 = ((f32[64,2,2,8,128]{4,3,2,1,0:T(8,128)}), f32[64,2,2,8,128]{4,3,2,1,0:T(8,128)S(1)}, u32[]{:S(2)}, u32[]{:S(2)}) async-start(f32[64,2,2,8,128]{4,3,2,1,0:T(8,128)} %bitcast.5), calls=%async_computation.1 | async-start | bytes 2097152 | tf_op jit(solution)/shard_map/all_to_all | solution.py:244
